TPU v7x, 256 devices: a whole 4x4x8 slice. The times are simulated.
256 devices in a mesh: frames: 64 (over y, z, x_hi), band: 4 (over x_lo, core).
Axes of the slice: x: 4 (x_hi: 2, x_lo: 2; x = x_hi * 2 + x_lo), y: 4, z: 8, core: 2. Of those that a mesh axis runs over, the one named last changes fastest.
Arguments:
- tokens: bfloat16 [128, 1024, 1024], P('frames', 'band'), may hold values from -6 to 6
- norm_space: float32 [1024], replicated, may hold values from 0.5 to 1.5
- query_space: bfloat16 [1024, 1024], replicated, may hold values from -0.1875 to 0.1875
- keyval_space: bfloat16 [1024, 512], replicated, may hold values from -0.1875 to 0.1875
- out_space: bfloat16 [1024, 1024], replicated, may hold values from -0.1875 to 0.1875
- qk_space: float32 [2, 64], replicated, may hold values from 0.7 to 7
- norm_time: float32 [1024], replicated, may hold values from 0.5 to 1.5
- query_time: bfloat16 [1024, 1024], replicated, may hold values from -0.1875 to 0.1875
- keyval_time: bfloat16 [1024, 512], replicated, may hold values from -0.1875 to 0.1875
- out_time: bfloat16 [1024, 1024], replicated, may hold values from -0.1875 to 0.1875
- qk_time: float32 [2, 64], replicated, may hold values from 0.7 to 7
Outputs:
- mixed: bfloat16 [128, 1024, 1024], P('frames', 'band')
All inputs are finite; a program needn't handle non-finite values.
Results may differ from a plain program's by a relative error of at most 0.025.
The roundings to bfloat16 on the way count: a program that leaves them out, or rounds other values in their place, can miss the bound.
Values may be sent and summed in bfloat16 or wider, within the bound.
A program may use at most 128 MiB of HBM per device.

v0:
```python
import jax
import jax.numpy as jnp
from jax import lax
from jax.sharding import PartitionSpec as P

HEADS = 16
KV_HEADS = 4
HEAD_DIM = 64


def rms_rows(values, gain):
    values = values.astype(jnp.float32)
    scaled = lax.rsqrt(jnp.mean(values * values, axis=-1, keepdims=True) + 1e-06)
    return values * scaled * gain


def project(hidden, w_query, w_keyval, qk_gain):
    row_count = hidden.shape[0]
    queries = jnp.dot(hidden, w_query, preferred_element_type=jnp.float32)
    keyval = jnp.dot(hidden, w_keyval, preferred_element_type=jnp.float32)
    queries = rms_rows(queries.reshape(row_count, HEADS, HEAD_DIM), qk_gain[0])
    key_part = keyval[:, : KV_HEADS * HEAD_DIM].reshape(row_count, KV_HEADS, HEAD_DIM)
    key_rows = rms_rows(key_part, qk_gain[1])
    values = keyval[:, KV_HEADS * HEAD_DIM :]
    return (
        queries.reshape(row_count, -1).astype(jnp.bfloat16),
        key_rows.reshape(row_count, -1).astype(jnp.bfloat16),
        values.astype(jnp.bfloat16),
    )


def attend(queries, key_rows, values, causal_mask):
    query_count = queries.shape[0]
    key_count = key_rows.shape[0]
    groups = HEADS // KV_HEADS
    grouped = queries.reshape(query_count, KV_HEADS, groups, HEAD_DIM)
    key_heads = key_rows.reshape(key_count, KV_HEADS, HEAD_DIM)
    value_heads = values.reshape(key_count, KV_HEADS, HEAD_DIM)
    scores = jnp.einsum(
        "nkgd,mkd->kgnm", grouped, key_heads, preferred_element_type=jnp.float32
    ) * HEAD_DIM ** (-0.5)
    if causal_mask is not None:
        scores = jnp.where(causal_mask, scores, -jnp.inf)
    largest = jnp.max(scores, axis=-1, keepdims=True)
    expos = jnp.exp(scores - largest)
    totals = jnp.sum(expos, axis=-1)
    weights = expos.astype(jnp.bfloat16)
    summed = jnp.einsum("kgnm,mkd->nkgd", weights, value_heads, preferred_element_type=jnp.float32)
    summed = summed / jnp.transpose(totals, (2, 0, 1))[..., None]
    return summed.reshape(query_count, HEADS * HEAD_DIM).astype(jnp.bfloat16)


def body(
    tokens,
    norm_space,
    query_space,
    keyval_space,
    out_space,
    qk_space,
    norm_time,
    query_time,
    keyval_time,
    out_time,
    qk_time,
):
    frames_here, rows_here, model_width = tokens.shape
    flat_tokens = tokens.reshape(frames_here * rows_here, model_width)
    normed = rms_rows(flat_tokens, norm_space).astype(jnp.bfloat16)
    queries, key_rows, values = project(normed, query_space, keyval_space, qk_space)
    queries = queries.reshape(frames_here, rows_here, -1)
    key_rows = key_rows.reshape(frames_here, rows_here, -1)
    values = values.reshape(frames_here, rows_here, -1)
    all_keys, all_values = (
        lax.all_gather(key_rows, "band", axis=1, tiled=True),
        lax.all_gather(values, "band", axis=1, tiled=True),
    )

    def space_frame(pieces):
        frame_q, frame_k, frame_v = pieces
        return attend(frame_q, frame_k, frame_v, None)

    attended = lax.map(space_frame, (queries, all_keys, all_values))
    attended = attended.reshape(frames_here * rows_here, HEADS * HEAD_DIM)
    update = jnp.dot(attended, out_space, preferred_element_type=jnp.float32)
    stream = (flat_tokens.astype(jnp.float32) + update).astype(jnp.bfloat16)
    normed_time = rms_rows(stream, norm_time).astype(jnp.bfloat16)
    time_q, time_k, time_v = project(normed_time, query_time, keyval_time, qk_time)
    time_q, time_k, time_v = (
        lax.all_to_all(
            time_q.reshape(frames_here, rows_here, -1),
            "frames",
            split_axis=1,
            concat_axis=0,
            tiled=True,
        ),
        lax.all_to_all(
            time_k.reshape(frames_here, rows_here, -1),
            "frames",
            split_axis=1,
            concat_axis=0,
            tiled=True,
        ),
        lax.all_to_all(
            time_v.reshape(frames_here, rows_here, -1),
            "frames",
            split_axis=1,
            concat_axis=0,
            tiled=True,
        ),
    )
    frame_total, local_positions = (time_q.shape[0], time_q.shape[1])
    order = jnp.arange(frame_total, dtype=jnp.int32)
    causal_mask = order[:, None] >= order[None, :]
    time_att = jax.vmap(lambda qq, kk, vv: attend(qq, kk, vv, causal_mask))(
        jnp.swapaxes(time_q, 0, 1), jnp.swapaxes(time_k, 0, 1), jnp.swapaxes(time_v, 0, 1)
    )
    time_att = jnp.swapaxes(time_att, 0, 1)
    returned = lax.all_to_all(time_att, "frames", split_axis=0, concat_axis=1, tiled=True)
    returned = returned.reshape(frames_here * rows_here, HEADS * HEAD_DIM)
    update_time = jnp.dot(returned, out_time, preferred_element_type=jnp.float32)
    mixed = (stream.astype(jnp.float32) + update_time).astype(jnp.bfloat16)
    return mixed.reshape(frames_here, rows_here, model_width)


def solution(mesh):
    placed = (P("frames", "band", None), P(), P(), P(), P(), P(), P(), P(), P(), P(), P())
    return jax.shard_map(
        body, mesh=mesh, in_specs=placed, out_specs=P("frames", "band", None), check_vma=False
    )
```

profile of v0, /device:TPU:1, one launch (start us, length us, event | category | flops | bytes accessed | tf_op | source)
XLA Modules:
  0.0 278.1 jit_solution(18135022672285937646)
XLA Ops:
  6.5 1.7 fusion.21
  8.2 1.5 fusion.25
  9.8 0.7 fusion.41
  10.5 1.0 copy-done.3
  12.2 1.1 multiply_convert_fusion.3
  13.4 0.8 copy.44
  14.3 1.1 slice.49
  15.3 0.8 copy.41
  16.2 4.0 %copy.45 = bf16[1024,1024]{0,1:T(8,128)(2,1)} copy(bf16[1024,1024]{1,0:T(8,128)(2,1)} %param.15) | data formatting | bytes 4194304 | tf_op args[2]
  20.6 1.3 copy-done.2
  21.9 1.3 multiply_reduce_fusion
  23.2 0.5 multiply_convert_fusion.1
  23.7 1.1 convert_element_type.83
  24.8 2.3 copy.46
  27.3 14.2 %all-gather.5.cloned.1.call-done = bf16[2,1024,256]{1,2,0:T(8,128)(2,1)} async-done(((bf16[2,256,256]{1,2,0:T(8,128)(2,1)}), bf16[2,1024,256]{1,2,0:T(8,128)(2,1)}) %all-gather.5.cloned.1.call-update) | async-done | bytes 1048592 | tf_op jit(solution)/shard_map/all_gather | solution.py:74
  41.5 26.5 %all-gather.3.cloned.1.call-done = bf16[2,1024,256]{1,2,0:T(8,128)(2,1)} async-done(((bf16[2,256,256]{1,2,0:T(8,128)(2,1)}), bf16[2,1024,256]{1,2,0:T(8,128)(2,1)}) %all-gather.3.cloned.1.call-update) | async-done | bytes 1048592 | tf_op jit(solution)/shard_map/all_gather | solution.py:75
  68.1 57.7 %while.10 = (s32[]{:T(128)}, bf16[2,256,1024]{2,1,0:T(8,128)(2,1)}, bf16[2,1024,256]{1,2,0:T(8,128)(2,1)}, bf16[2,1024,256]{1,2,0:T(8,128)(2,1)}, bf16[2,256,1024]{1,2,0:T(8,128)(2,1)}, /*index=5*/s32[]{:T(128)}) while((s32[]{:T(128)}, bf16[2,256,1024]{2,1,0:T(8,128)(2,1)}, bf16[2,1024,256]{1,2,0:T(8,128)(2,1)}, ...), condition=%wide.region_6.7_spmd, body=%wide.region_3.6_spmd.sunk | while | flops 1107812352 | bytes 57754188 | solution.py:82
  68.1 1.3 constant_dynamic-slice_fusion.5
  69.3 1.1 constant_dynamic-slice_fusion.6
  70.4 8.1 %bitcast_reduce_fusion.5 = (f32[4,4,256]{2,1,0:T(4,128)S(1)}, f32[4,1024,256,4]{2,1,3,0:T(8,128)}) fusion(bf16[1024,4,64,1]{0,2,3,1:T(8,128)(2,1)S(1)} %bitcast.167, bf16[256,4,4,64]{0,3,2,1:T(8,128)(2,1)S(1)} %bitcast.168), kind=kOutput, calls=%fused_computation.1.clone.1 | convolution fusion | flops 545255424 | bytes 17842176 | tf_op jit(solution)/shard_map/while/body/eval_jaxpr/nkgd,mkd->kgnm/dot_general | solution.py:39
  78.5 8.6 %fusion.67 = f32[4,4,256]{2,1,0:T(4,128)S(1)} fusion(f32[4,1024,256,4]{2,1,3,0:T(8,128)} %get-tuple-element.113, f32[4,4,256]{2,1,0:T(4,128)S(1)} %get-tuple-element.114), kind=kLoop, calls=%fused_computation.3.clone.1 | loop fusion | flops 12578816 | bytes 16809984 | tf_op jit(solution)/shard_map/while/body/eval_jaxpr/reduce_sum | solution.py:46
  87.1 8.7 %divide_convert_fusion.2 = bf16[256,4,4,64]{0,3,2,1:T(8,128)(2,1)S(1)} fusion(bf16[1024,4,64,1]{0,2,3,1:T(8,128)(2,1)S(1)} %bitcast.165, f32[4,1024,256,4]{2,1,3,0:T(8,128)} %get-tuple-element.113, f32[4,4,256]{2,1,0:T(4,128)S(1)} %get-tuple-element.114, f32[256,4,4]{0,2,1:T(4,128)S(1)} %bitcast.176), kind=kOutput, calls=%fused_computation.7.clone.1 | convolution fusion | flops 549978112 | bytes 17858560 | tf_op jit(solution)/shard_map/while/body/eval_jaxpr/kgnm,mkd->nkgd/dot_general | solution.py:48
  96.1 0.8 constant_dynamic-update-slice_fusion.2
  96.9 1.3 constant_dynamic-slice_fusion.5
  98.2 1.1 constant_dynamic-slice_fusion.6
  99.3 8.1 %bitcast_reduce_fusion.5 = (f32[4,4,256]{2,1,0:T(4,128)S(1)}, f32[4,1024,256,4]{2,1,3,0:T(8,128)}) fusion(bf16[1024,4,64,1]{0,2,3,1:T(8,128)(2,1)S(1)} %bitcast.167, bf16[256,4,4,64]{0,3,2,1:T(8,128)(2,1)S(1)} %bitcast.168), kind=kOutput, calls=%fused_computation.1.clone.1 | convolution fusion | flops 545255424 | bytes 17842176 | tf_op jit(solution)/shard_map/while/body/eval_jaxpr/nkgd,mkd->kgnm/dot_general | solution.py:39
  107.4 8.6 %fusion.67 = f32[4,4,256]{2,1,0:T(4,128)S(1)} fusion(f32[4,1024,256,4]{2,1,3,0:T(8,128)} %get-tuple-element.113, f32[4,4,256]{2,1,0:T(4,128)S(1)} %get-tuple-element.114), kind=kLoop, calls=%fused_computation.3.clone.1 | loop fusion | flops 12578816 | bytes 16809984 | tf_op jit(solution)/shard_map/while/body/eval_jaxpr/reduce_sum | solution.py:46
  116.0 8.7 %divide_convert_fusion.2 = bf16[256,4,4,64]{0,3,2,1:T(8,128)(2,1)S(1)} fusion(bf16[1024,4,64,1]{0,2,3,1:T(8,128)(2,1)S(1)} %bitcast.165, f32[4,1024,256,4]{2,1,3,0:T(8,128)} %get-tuple-element.113, f32[4,4,256]{2,1,0:T(4,128)S(1)} %get-tuple-element.114, f32[256,4,4]{0,2,1:T(4,128)S(1)} %bitcast.176), kind=kOutput, calls=%fused_computation.7.clone.1 | convolution fusion | flops 549978112 | bytes 17858560 | tf_op jit(solution)/shard_map/while/body/eval_jaxpr/kgnm,mkd->nkgd/dot_general | solution.py:48
  124.9 0.8 constant_dynamic-update-slice_fusion.2
  125.7 3.6 %fusion.14 = (f32[512]{0:T(512)S(1)}, bf16[512,1024]{1,0:T(8,128)(2,1)S(1)}) fusion(bf16[512,1024]{1,0:T(8,128)(2,1)} %bitcast.194, bf16[1024,1024]{1,0:T(8,128)(2,1)} %param.17, bf16[2,256,1024]{2,1,0:T(8,128)(2,1)} %param.13), kind=kOutput, calls=%fused_computation.21 | convolution fusion | flops 1076887040 | bytes 5244928 | tf_op jit(solution)/shard_map/dot_general | solution.py:84
  129.4 0.8 fusion.35
  130.4 0.8 copy-done.4
  131.2 0.7 slice.48
  132.4 1.1 multiply_convert_fusion.2
  133.6 1.0 copy.53
  134.5 13.2 %all-to-all-start.1 = ((bf16[2,256,256]{2,0,1:T(2,128)(2,1)}), bf16[2,256,256]{2,0,1:T(2,128)(2,1)S(1)}, u32[]{:S(2)}, u32[]{:S(2)}) async-start(bf16[2,256,256]{2,0,1:T(2,128)(2,1)} %copy.53), calls=%async_computation.1 | async-start | bytes 524288 | tf_op jit(solution)/shard_map/all_to_all | solution.py:96
  147.7 4.5 %fusion.40 = (f32[512,1024]{1,0:T(8,128)}, f32[512,1024]{1,0:T(8,128)}) fusion(bf16[1024,1024]{1,0:T(8,128)(2,1)S(1)} %copy-done, bf16[512,1024]{1,0:T(8,128)(2,1)} %copy-done.15, f32[1024]{0:T(1024)S(1)} %copy-done.14, f32[512]{0:T(512)S(1)} %add_rsqrt_fusion.4), kind=kOutput, calls=%fused_computation.70 | convolution fusion | flops 1076363264 | bytes 7346176 | tf_op jit(solution)/shard_map/dot_general | solution.py:19
  152.2 2.9 %copy.56 = f32[512,1024]{0,1:T(8,128)} copy(f32[512,1024]{1,0:T(8,128)} %get-tuple-element.72) | data formatting | bytes 4194304 | tf_op jit(solution)/shard_map/mul | solution.py:13
  155.1 1.0 copy.48
  156.1 1.9 bitcast_reduce_fusion.1
  158.0 2.2 all-to-all-done.1
  160.1 10.1 %all-to-all-start = ((bf16[2,256,256]{2,0,1:T(2,128)(2,1)}), bf16[2,256,256]{2,0,1:T(2,128)(2,1)S(1)}, u32[]{:S(2)}, u32[]{:S(2)}) async-start(bf16[2,256,256]{2,0,1:T(2,128)(2,1)} %copy.48), calls=%async_computation | async-start | bytes 524288 | tf_op jit(solution)/shard_map/all_to_all | solution.py:103
  170.2 1.6 mul.223
  171.8 2.9 %copy.57 = f32[512,1024]{1,0:T(8,128)} copy(f32[512,1024]{0,1:T(8,128)} %bitcast.169) | data formatting | bytes 4194304 | tf_op jit(solution)/shard_map/mul | solution.py:14
  174.7 2.7 multiply_convert_fusion
  177.4 2.0 copy.58
  179.5 2.5 all-to-all-done
  182.0 0.7 copy-done.5
  182.7 9.9 %all-to-all-start.2 = ((bf16[2,256,1024]{2,0,1:T(2,128)(2,1)}), bf16[2,256,1024]{2,0,1:T(2,128)(2,1)S(1)}, u32[]{:S(2)}, u32[]{:S(2)}) async-start(bf16[2,256,1024]{2,0,1:T(2,128)(2,1)} %copy.58), calls=%async_computation.2 | async-start | bytes 2097152 | tf_op jit(solution)/shard_map/all_to_all | solution.py:89
  192.6 0.8 copy.54
  193.4 1.8 copy.55
  195.2 1.1 copy.49
  196.3 0.9 copy.50
  197.2 23.5 %all-to-all-done.2 = bf16[2,256,1024]{2,0,1:T(2,128)(2,1)S(1)} async-done(((bf16[2,256,1024]{2,0,1:T(2,128)(2,1)}), bf16[2,256,1024]{2,0,1:T(2,128)(2,1)S(1)}, u32[]{:S(2)}, u32[]{:S(2)}) %all-to-all-start.2) | async-done | bytes 1048608 | tf_op jit(solution)/shard_map/all_to_all | solution.py:89
  220.7 1.5 copy.59
  222.2 1.9 copy.60
  224.1 0.8 fusion.13
  224.9 1.2 fusion.11
  226.1 2.1 fusion.20
  228.2 1.9 copy.62
  230.1 35.3 %all_to_all.69 = bf16[128,4,1024]{2,1,0:T(4,128)(2,1)S(1)} all-to-all(bf16[128,4,1024]{2,1,0:T(4,128)(2,1)S(1)} %bitcast.172), channel_id=1, replica_groups=mesh['frames'=64,'band'=4] {'frames'}, dimensions={0} | all-to-all | bytes 2097152 | tf_op jit(solution)/shard_map/all_to_all | solution.py:118
  265.4 0.4 copy.63
  265.8 1.1 reshape.171
  266.9 4.4 %fusion.17 = bf16[512,1024]{1,0:T(8,128)(2,1)} fusion(bf16[512,1024]{1,0:T(8,128)(2,1)} %copy-done.15, bf16[512,1024]{1,0:T(8,128)(2,1)} %reshape.171, bf16[1024,1024]{1,0:T(8,128)(2,1)} %param.22), kind=kOutput, calls=%fused_computation.24 | convolution fusion | flops 1075314688 | bytes 5242880 | tf_op jit(solution)/shard_map/dot_general | solution.py:120
  (62 shorter events, 2.5 us)
Async XLA Ops:
  6.5 141.2 %copy-start = (bf16[1024,1024]{1,0:T(8,128)(2,1)S(1)}, bf16[1024,1024]{1,0:T(8,128)(2,1)}, u32[]{:S(2)}) copy-start(bf16[1024,1024]{1,0:T(8,128)(2,1)} %param.20) | copy-start | bytes 6291460
  6.5 3.2 %copy-start.12 = (bf16[1024,512]{1,0:T(8,128)(2,1)S(1)}, bf16[1024,512]{1,0:T(8,128)(2,1)}, u32[]{:S(2)}) copy-start(bf16[1024,512]{1,0:T(8,128)(2,1)} %param.16) | copy-start | bytes 3145732
  6.5 35.0 %all-gather.5.cloned.1.call-start = ((), (), s32[]{:S(2)}) async-start(), calls=%async_computation.5 | async-start | bytes 1310720 | tf_op jit(solution)/shard_map/all_gather | solution.py:74
  10.5 1.0 copy-start.3
  11.5 0.7 copy-start.10
  14.2 53.8 %all-gather.3.cloned.1.call-start = ((), (), s32[]{:S(2)}) async-start(), calls=%async_computation.4 | async-start | bytes 1310720 | tf_op jit(solution)/shard_map/all_gather | solution.py:75
  16.2 4.1 %copy-start.1 = (bf16[2,256,1024]{2,1,0:T(8,128)(2,1)S(1)}, bf16[2,256,1024]{2,1,0:T(8,128)(2,1)}, u32[]{:S(2)}) copy-start(bf16[2,256,1024]{2,1,0:T(8,128)(2,1)} %param.13) | copy-start | bytes 3145732
  16.2 4.0 %copy-start.9 = (f32[1024]{0:T(1024)S(1)}, f32[1024]{0:T(1024)}, u32[]{:S(2)}) copy-start(f32[1024]{0:T(1024)} %param.14) | copy-start | bytes 12292
  20.3 1.6 copy-start.2
  23.7 3.5 %copy-start.11 = (f32[2,64]{1,0:T(2,128)S(1)}, f32[2,64]{1,0:T(2,128)}, u32[]{:S(2)}) copy-start(f32[2,64]{1,0:T(2,128)} %param.23) | copy-start | bytes 1540
  125.7 3.7 %copy-start.13 = (bf16[1024,512]{1,0:T(8,128)(2,1)S(1)}, bf16[1024,512]{1,0:T(8,128)(2,1)}, u32[]{:S(2)}) copy-start(bf16[1024,512]{1,0:T(8,128)(2,1)} %param.21) | copy-start | bytes 3145732
  125.7 3.7 %copy-start.14 = (f32[1024]{0:T(1024)S(1)}, f32[1024]{0:T(1024)}, u32[]{:S(2)}) copy-start(f32[1024]{0:T(1024)} %param.19) | copy-start | bytes 12292
  129.4 1.0 copy-start.15
  130.2 1.0 copy-start.4
  134.5 25.6 %all-to-all-start.1 = ((bf16[2,256,256]{2,0,1:T(2,128)(2,1)}), bf16[2,256,256]{2,0,1:T(2,128)(2,1)S(1)}, u32[]{:S(2)}, u32[]{:S(2)}) async-start(bf16[2,256,256]{2,0,1:T(2,128)(2,1)} %copy.53), calls=%async_computation.1 | async-start | bytes 524288 | tf_op jit(solution)/shard_map/all_to_all | solution.py:96
  152.2 2.9 %copy-start.6 = (bf16[512,256]{1,0:T(8,128)(2,1)S(1)}, bf16[512,256]{1,0:T(8,128)(2,1)}, u32[]{:S(2)}) copy-start(bf16[512,256]{1,0:T(8,128)(2,1)} %slice.48) | copy-start | bytes 786436
  160.1 21.9 %all-to-all-start = ((bf16[2,256,256]{2,0,1:T(2,128)(2,1)}), bf16[2,256,256]{2,0,1:T(2,128)(2,1)S(1)}, u32[]{:S(2)}, u32[]{:S(2)}) async-start(bf16[2,256,256]{2,0,1:T(2,128)(2,1)} %copy.48), calls=%async_computation | async-start | bytes 524288 | tf_op jit(solution)/shard_map/all_to_all | solution.py:103
  182.0 0.7 copy-start.5
  182.7 37.9 %all-to-all-start.2 = ((bf16[2,256,1024]{2,0,1:T(2,128)(2,1)}), bf16[2,256,1024]{2,0,1:T(2,128)(2,1)S(1)}, u32[]{:S(2)}, u32[]{:S(2)}) async-start(bf16[2,256,1024]{2,0,1:T(2,128)(2,1)} %copy.58), calls=%async_computation.2 | async-start | bytes 2097152 | tf_op jit(solution)/shard_map/all_to_all | solution.py:89
  220.7 3.4 %copy-start.7 = (bf16[4,128,256]{1,2,0:T(8,128)(2,1)S(1)}, bf16[4,128,256]{1,2,0:T(8,128)(2,1)}, u32[]{:S(2)}) copy-start(bf16[4,128,256]{1,2,0:T(8,128)(2,1)} %copy.55) | copy-start | bytes 786436
  224.9 1.2 copy-start.8
Sparse Core Ops, SparseCore 0:
  14.3 27.1 all-gather.4
  43.3 24.7 all-gather.2
where the time goes:
time: 280 us; the launch traced here: 278 us
  waiting for transfers between devices  68.9 us (25%)
  matrix products  51.9 us (19%)
  local copies, waits for them, and re-layouts  45.6 us (16%)
  blocking collectives  35.3 us (13%)
  starting transfers between devices  33.1 us (12%)
  other arithmetic  29.5 us (11%)
  between operations  13.8 us (5%)
    all_to_all x1, blocking collectives, body(): lax.all_to_all(time_att, 'frames', split_axis=0, concat_axis=1, tiled=True)  35.3 us
    all_gather x1, waiting for transfers between devices, body(): lax.all_gather(values, 'band', axis=1, tiled=True)  26.5 us
    all_to_all x1, waiting for transfers between devices, body(): lax.all_to_all(time_q.reshape(frames_here, rows_here, -1), 'frames', spli...  23.5 us
    dot_general x3, matrix products, attend(): jnp.einsum('kgnm,mkd->nkgd', weights, value_heads, preferred_element_type...  19.6 us
    reduce_sum x3, other arithmetic, attend(): totals = jnp.sum(expos, axis=-1)  18.3 us
    dot_general x3, matrix products, attend(): jnp.einsum('nkgd,mkd->kgnm', grouped, key_heads, preferred_element_type=j...  17 us
    all_gather x1, waiting for transfers between devices, body(): lax.all_gather(key_rows, 'band', axis=1, tiled=True)  14.2 us
    all_to_all x1, starting transfers between devices, body(): lax.all_to_all(time_k.reshape(frames_here, rows_here, -1), 'frames', spli...  13.2 us
  transfers between devices with their start and end apart: 5, of which 5 were waited for; matrix products, arithmetic and copies ran while one was open for 13% of the time, Pallas kernels for 0%

commit v1 on v0

v1 whole, which is shorter than its diff:
```python
import functools

import jax
import jax.numpy as jnp
from jax import lax
from jax.experimental import pallas as pl
from jax.experimental.pallas import tpu as pltpu
from jax.sharding import PartitionSpec as P

HEADS = 16
KV_HEADS = 4
HEAD_DIM = 64
D = 1024
ROWS = 256
PEERS = 64
POS = 4
MESH = pl.DeviceIdType.MESH
F32 = jnp.float32
BF16 = jnp.bfloat16
EXP_SCALE = 0.125 * 1.4426950408889634


def lane_half(shape):
    return lax.broadcasted_iota(jnp.int32, shape, len(shape) - 1) // HEAD_DIM


def rms_pair(tile, gain, ones_block):
    squares = tile * tile
    high = squares.astype(BF16)
    low = (squares - high.astype(F32)).astype(BF16)
    mean = jnp.dot(jnp.concatenate([high, low], axis=1), ones_block, preferred_element_type=F32)
    return tile * lax.rsqrt(mean + 1e-06) * gain


def head_queries(tile, pair):
    parity = (pair // 2) % 2
    here = lane_half(tile.shape) == parity
    turned = pltpu.roll(tile, HEAD_DIM, 1)
    first, second = (tile, turned) if parity == 0 else (turned, tile)
    zero = jnp.zeros_like(tile)
    return jnp.where(here, first, zero).astype(BF16), jnp.where(here, second, zero).astype(BF16)


def join_heads(first, second, parity):
    first = first * (1.0 / pltpu.roll(first, HEAD_DIM, 1))
    second = second * (1.0 / pltpu.roll(second, HEAD_DIM, 1))
    low = lane_half(first.shape) == 0
    if parity == 0:
        return jnp.where(low, first, pltpu.roll(second, HEAD_DIM, 1))
    return jnp.where(low, pltpu.roll(first, HEAD_DIM, 1), second)


def with_ones(tile, parity):
    return jnp.where(lane_half(tile.shape) == parity, tile, jnp.ones_like(tile))


def pack_rows(left, right):
    left = left.reshape(32, 8, 128)
    right = right.reshape(32, 8, 128)
    low = lax.broadcasted_iota(jnp.int32, left.shape, 1) < 4
    even = jnp.where(low, left, pltpu.roll(right, 4, 1))
    odd = jnp.where(low, pltpu.roll(left, 4, 1), right)
    return jnp.stack([even, odd], axis=1).reshape(PEERS, 8, 128)


def unpack_rows(packed):
    packed = packed.reshape(32, 2, 8, 128)
    even, odd = packed[:, 0], packed[:, 1]
    low = lax.broadcasted_iota(jnp.int32, even.shape, 1) < 4
    left = jnp.where(low, even, pltpu.roll(odd, 4, 1))
    right = jnp.where(low, pltpu.roll(even, 4, 1), odd)
    return left.reshape(ROWS, 128), right.reshape(ROWS, 128)


def gain_row(ref):
    return jnp.concatenate([ref[k : k + 1, :] for k in range(8)], axis=1)


def normalise(values, gain):
    return (values * lax.rsqrt(jnp.mean(values * values, axis=-1, keepdims=True) + 1e-06) * gain).astype(BF16)


def kernel(
    tok_hbm, ns_ref, wqs_hbm, wkvs_hbm, wos_hbm, qks_ref, nt_ref, wqt_hbm, wkvt_hbm, wot_hbm, qkt_ref,
    out_hbm,
    tok, wqs, wkvs, wos, wqt, wkvt, wot,
    normed, queries, kv_all, keys_t, vals, att, send_buf, recv_buf,
    shuffle, stream_t, normed_t, queries_t, keys_time, vals_time, att_t, back_buf, home_buf, out_buf,
    load_sem, kv_send, kv_recv, a2a_send, a2a_recv, back_send, back_recv, out_sem,
):
    me = lax.axis_index("frames")
    band = lax.axis_index("band")
    core_peer = lax.bitwise_xor(band, 1)
    chip_peer = lax.bitwise_xor(band, 2)

    loads = {}
    for k, (name, src, dst) in enumerate(
        [("tok", tok_hbm, tok), ("wkvs", wkvs_hbm, wkvs), ("wqs", wqs_hbm, wqs), ("wos", wos_hbm, wos),
         ("wqt", wqt_hbm, wqt), ("wkvt", wkvt_hbm, wkvt), ("wot", wot_hbm, wot)]
    ):
        loads[name] = pltpu.make_async_copy(src, dst, load_sem.at[k])
        loads[name].start()

    barrier = pltpu.get_barrier_semaphore()

    def greet(k, carry):
        pl.semaphore_signal(barrier, inc=1, device_id={"frames": lax.rem(me + k, PEERS)}, device_id_type=MESH)
        return carry

    lax.fori_loop(1, PEERS, greet, 0)
    for peer in (core_peer, chip_peer):
        pl.semaphore_signal(barrier, inc=1, device_id={"band": peer}, device_id_type=MESH)

    row = lax.broadcasted_iota(jnp.int32, (256, 128), 0)
    col = lax.broadcasted_iota(jnp.int32, (256, 128), 1)
    ones_block = jnp.where((row // HEAD_DIM) % 2 == col // HEAD_DIM, 1.0 / HEAD_DIM, 0.0).astype(BF16)

    def pair_gain(ref, k):
        return jnp.concatenate([ref[k : k + 1, :], ref[k : k + 1, :]], axis=1)

    loads["tok"].wait()
    gain_space = gain_row(ns_ref)

    def norm_rows(k, carry):
        rows = pl.ds(pl.multiple_of(k * 64, 64), 64)
        normed[rows, :] = normalise(tok[rows, :].astype(F32), gain_space)
        return carry

    lax.fori_loop(0, 2 * ROWS // 64, norm_rows, 0)

    def kv_copy(frame, slot, kind, peer):
        return pltpu.make_async_remote_copy(
            src_ref=kv_all.at[frame, slot], dst_ref=kv_all.at[frame, slot],
            send_sem=kv_send.at[frame, kind], recv_sem=kv_recv.at[frame, kind],
            device_id={"band": peer}, device_id_type=MESH)

    loads["wkvs"].wait()
    key_gain = pair_gain(qks_ref, 1)
    for frame in range(2):
        rows = slice(frame * ROWS, (frame + 1) * ROWS)
        part = jnp.dot(normed[rows, :], wkvs[...], preferred_element_type=F32)
        for t in range(2):
            tile = part[:, t * 128 : (t + 1) * 128]
            kv_all[frame, band, :, t * 128 : (t + 1) * 128] = rms_pair(tile, key_gain, ones_block).astype(BF16)
        kv_all[frame, band, :, 256:512] = part[:, 256:].astype(BF16)
        if frame == 0:
            pl.semaphore_wait(barrier, PEERS - 1 + 2)
        kv_copy(frame, band, 1, chip_peer).start()
        kv_copy(frame, band, 0, core_peer).start()

    loads["wqs"].wait()
    query_gain = pair_gain(qks_ref, 0)
    for n in range(4):
        part = jnp.dot(normed[...], wqs[:, n * 256 : (n + 1) * 256], preferred_element_type=F32)
        for k in range(2):
            pair = 2 * n + k
            tile = rms_pair(part[:, k * 128 : (k + 1) * 128], query_gain, ones_block)
            first, second = head_queries(tile, pair)
            queries[2 * pair] = first
            queries[2 * pair + 1] = second

    def forward(frame):
        kv_copy(frame, chip_peer, 1, chip_peer).wait_recv()
        kv_copy(frame, chip_peer, 2, core_peer).start()

    def space_frame(frame):
        kv_copy(frame, core_peer, 0, core_peer).wait_recv()
        kv_copy(frame, lax.bitwise_xor(band, 3), 2, core_peer).wait_recv()
        for src in range(4):
            at = slice(src * ROWS, (src + 1) * ROWS)
            for t in range(2):
                keys_t[t, :, at] = kv_all[frame, src, :, t * 128 : (t + 1) * 128].T
                value_tile = kv_all[frame, src, :, 256 + t * 128 : 256 + (t + 1) * 128]
                for parity in range(2):
                    vals[2 * t + parity, at, :] = with_ones(value_tile, parity)

        def one_kv(t, carry):
            for parity in range(2):
                for k in range(2):
                    pair = 4 * t + 2 * parity + k
                    done = []
                    for h in range(2):
                        q = queries[2 * pair + h, frame * ROWS : (frame + 1) * ROWS, :]
                        scores = jnp.dot(q, keys_t[t], preferred_element_type=F32)
                        largest = jnp.max(scores, axis=-1, keepdims=True)
                        weights = jnp.exp2((scores - largest) * EXP_SCALE).astype(BF16)
                        done.append(jnp.dot(weights, vals[2 * t + parity], preferred_element_type=F32))
                    att[pair] = join_heads(done[0], done[1], parity).astype(BF16)
            return carry

        lax.fori_loop(0, 2, one_kv, 0)

    def block_columns(left_ref, w_ref, n):
        left = jnp.concatenate([left_ref[k] for k in range(8)], axis=1)
        return jnp.dot(left, w_ref[:, n * 256 : (n + 1) * 256], preferred_element_type=F32)

    def send_all(buf, dst, frame, send_sem, recv_sem):
        def send(k, carry):
            peer = lax.rem(me + k, PEERS)
            pltpu.make_async_remote_copy(
                src_ref=buf.at[frame, peer], dst_ref=dst.at[frame, me],
                send_sem=send_sem.at[frame], recv_sem=recv_sem.at[frame],
                device_id={"frames": peer}, device_id_type=MESH).start()
            return carry

        lax.fori_loop(1, PEERS, send, 0)
        dst[frame, me] = buf[frame, me]

    def all_of(buf, dst, frame, send_sem, recv_sem):
        return pltpu.make_async_remote_copy(
            src_ref=buf.at[frame, pl.ds(0, PEERS - 1)], dst_ref=dst.at[frame, pl.ds(0, PEERS - 1)],
            send_sem=send_sem.at[frame], recv_sem=recv_sem.at[frame],
            device_id={"frames": me}, device_id_type=MESH)

    def out_space(frame):
        rows = slice(frame * ROWS, (frame + 1) * ROWS)
        for n in range(2):
            packs = []
            for m in (n, n + 2):
                at = slice(m * 256, (m + 1) * 256)
                stream = tok[rows, at].astype(F32) + block_columns(att, wos, m)
                stream = stream.astype(BF16).astype(F32)
                packs.append(pack_rows(stream[:, :128], stream[:, 128:]))
            send_buf[frame, :, :, n * 128 : (n + 1) * 128] = jnp.concatenate(packs, axis=1).astype(BF16)
        send_all(send_buf, recv_buf, frame, a2a_send, a2a_recv)

    forward(0)
    space_frame(0)
    forward(1)
    loads["wos"].wait()
    out_space(0)
    space_frame(1)
    out_space(1)

    gain_time = gain_row(nt_ref)
    query_gain_t = pair_gain(qkt_ref, 0)
    key_gain_t = pair_gain(qkt_ref, 1)
    for name in ("wqt", "wkvt", "wot"):
        loads[name].wait()

    def arrive(frame):
        all_of(send_buf, recv_buf, frame, a2a_send, a2a_recv).wait_recv()
        for n in range(2):
            pack = recv_buf[frame, :, :, n * 128 : (n + 1) * 128].astype(F32)
            for half, m in enumerate((n, n + 2)):
                left, right = unpack_rows(pack[:, half * 8 : (half + 1) * 8, :])
                shuffle[2 * m] = left
                shuffle[2 * m + 1] = right
        for j in range(POS):
            rows = slice(j * 64, (j + 1) * 64)
            values = jnp.concatenate([shuffle[k, pl.ds(j, 64, stride=4), :] for k in range(8)], axis=1)
            stream_t[frame, rows, :] = values.astype(BF16)
            normed_t[rows, :] = normalise(values, gain_time)
        hidden = normed_t[...]
        part = jnp.dot(hidden, wkvt[...], preferred_element_type=F32)
        keep = slice(frame * 64, (frame + 1) * 64)
        for t in range(2):
            tile = rms_pair(part[:, t * 128 : (t + 1) * 128], key_gain_t, ones_block).astype(BF16)
            value_tile = part[:, 256 + t * 128 : 256 + (t + 1) * 128].astype(BF16)
            for j in range(POS):
                rows = slice(j * 64, (j + 1) * 64)
                keys_time[j, t, keep, :] = tile[rows]
                for parity in range(2):
                    vals_time[j, 2 * t + parity, keep, :] = with_ones(value_tile[rows], parity)
        for n in range(4):
            part = jnp.dot(hidden, wqt[:, n * 256 : (n + 1) * 256], preferred_element_type=F32)
            for k in range(2):
                pair = 2 * n + k
                tile = rms_pair(part[:, k * 128 : (k + 1) * 128], query_gain_t, ones_block)
                first, second = head_queries(tile, pair)
                for j in range(POS):
                    rows = slice(j * 64, (j + 1) * 64)
                    queries_t[frame, j, 2 * pair] = first[rows]
                    queries_t[frame, j, 2 * pair + 1] = second[rows]

    def time_half(frame):
        q_frame = 2 * lax.broadcasted_iota(jnp.int32, (64, 128), 0) + frame
        k_row = lax.broadcasted_iota(jnp.int32, (64, 128), 1)
        allowed = q_frame >= 2 * (k_row % 64) + k_row // 64

        def position(j, carry):
            rows = pl.ds(pl.multiple_of(j * 64, 64), 64)
            for t in range(2):
                q = queries_t[frame, j, 8 * t : 8 * (t + 1)].reshape(512, 128)
                scores = lax.dot_general(q, keys_time[j, t], (((1,), (1,)), ((), ())), preferred_element_type=F32)
                scores = jnp.where(allowed[None], scores.reshape(8, 64, 128), -1e30)
                largest = jnp.max(scores, axis=-1, keepdims=True)
                weights = jnp.exp2((scores - largest) * EXP_SCALE).astype(BF16)
                for parity in range(2):
                    mine = weights[4 * parity : 4 * parity + 4].reshape(256, 128)
                    done = jnp.dot(mine, vals_time[j, 2 * t + parity], preferred_element_type=F32)
                    for k in range(2):
                        pair = 4 * t + 2 * parity + k
                        att_t[pair, rows, :] = join_heads(
                            done[k * 128 : k * 128 + 64], done[k * 128 + 64 : k * 128 + 128], parity
                        ).astype(BF16)
            return carry

        lax.fori_loop(0, POS, position, 0)
        for n in range(4):
            at = slice(n * 256, (n + 1) * 256)
            mixed = stream_t[frame, :, at].astype(F32) + block_columns(att_t, wot, n)
            mixed = mixed.astype(BF16).astype(F32)
            for j in range(POS):
                for half in range(2):
                    shuffle[2 * n + half, pl.ds(j, 64, stride=4), :] = mixed[
                        j * 64 : (j + 1) * 64, half * 128 : (half + 1) * 128]
        for n in range(2):
            packs = [pack_rows(shuffle[2 * m], shuffle[2 * m + 1]) for m in (n, n + 2)]
            back_buf[frame, :, :, n * 128 : (n + 1) * 128] = jnp.concatenate(packs, axis=1).astype(BF16)
        send_all(back_buf, home_buf, frame, back_send, back_recv)

    arrive(0)
    arrive(1)
    time_half(0)
    time_half(1)

    def finish(frame):
        all_of(back_buf, home_buf, frame, back_send, back_recv).wait_recv()
        for n in range(2):
            pack = home_buf[frame, :, :, n * 128 : (n + 1) * 128].astype(F32)
            for half, m in enumerate((n, n + 2)):
                left, right = unpack_rows(pack[:, half * 8 : (half + 1) * 8, :])
                out_buf[frame, :, m * 256 : m * 256 + 128] = left.astype(BF16)
                out_buf[frame, :, m * 256 + 128 : (m + 1) * 256] = right.astype(BF16)
        copy = pltpu.make_async_copy(out_buf.at[frame], out_hbm.at[frame], out_sem.at[frame])
        copy.start()
        return copy

    copies = [finish(0), finish(1)]
    for frame in range(2):
        kv_copy(frame, band, 0, core_peer).wait_send()
        kv_copy(frame, band, 1, chip_peer).wait_send()
        kv_copy(frame, chip_peer, 2, core_peer).wait_send()
        all_of(send_buf, recv_buf, frame, a2a_send, a2a_recv).wait_send()
        all_of(back_buf, home_buf, frame, back_send, back_recv).wait_send()
        copies[frame].wait()


def body(tokens, norm_space, query_space, keyval_space, out_space, qk_space,
         norm_time, query_time, keyval_time, out_time, qk_time):
    frames_here, rows_here, width = tokens.shape
    any_spec = pl.BlockSpec(memory_space=pl.ANY)
    vmem = pl.BlockSpec(memory_space=pltpu.VMEM)
    dma = pltpu.SemaphoreType.DMA
    return pl.pallas_call(
        kernel,
        out_shape=jax.ShapeDtypeStruct((frames_here, rows_here, width), BF16),
        in_specs=[any_spec, vmem, any_spec, any_spec, any_spec, vmem, vmem, any_spec, any_spec, any_spec, vmem],
        out_specs=any_spec,
        scratch_shapes=[
            pltpu.VMEM((2 * ROWS, D), BF16),
            pltpu.VMEM((D, D), BF16), pltpu.VMEM((D, 512), BF16), pltpu.VMEM((D, D), BF16),
            pltpu.VMEM((D, D), BF16), pltpu.VMEM((D, 512), BF16), pltpu.VMEM((D, D), BF16),
            pltpu.VMEM((2 * ROWS, D), BF16),
            pltpu.VMEM((HEADS, 2 * ROWS, 128), BF16),
            pltpu.VMEM((2, 4, ROWS, 512), BF16),
            pltpu.VMEM((2, 128, 4 * ROWS), BF16),
            pltpu.VMEM((KV_HEADS, 4 * ROWS, 128), BF16),
            pltpu.VMEM((8, ROWS, 128), BF16),
            pltpu.VMEM((2, PEERS, 16, 256), BF16),
            pltpu.VMEM((2, PEERS, 16, 256), BF16),
            pltpu.VMEM((8, ROWS, 128), F32),
            pltpu.VMEM((2, ROWS, D), BF16),
            pltpu.VMEM((ROWS, D), BF16),
            pltpu.VMEM((2, POS, HEADS, 64, 128), BF16),
            pltpu.VMEM((POS, 2, 128, 128), BF16),
            pltpu.VMEM((POS, KV_HEADS, 128, 128), BF16),
            pltpu.VMEM((8, ROWS, 128), BF16),
            pltpu.VMEM((2, PEERS, 16, 256), BF16),
            pltpu.VMEM((2, PEERS, 16, 256), BF16),
            pltpu.VMEM((2, ROWS, D), BF16),
            dma((7,)), dma((2, 3)), dma((2, 3)), dma((2,)), dma((2,)), dma((2,)), dma((2,)), dma((2,)),
        ],
        compiler_params=pltpu.CompilerParams(
            collective_id=0, has_side_effects=True, vmem_limit_bytes=58 * 2**20
        ),
        name="block",
    )(
        tokens.reshape(frames_here * rows_here, width), norm_space.reshape(8, 128), query_space, keyval_space,
        out_space, qk_space, norm_time.reshape(8, 128), query_time, keyval_time, out_time, qk_time,
    )


def solution(mesh):
    placed = (P("frames", "band", None), P(), P(), P(), P(), P(), P(), P(), P(), P(), P())
    return jax.shard_map(
        body, mesh=mesh, in_specs=placed, out_specs=P("frames", "band", None), check_vma=False
    )
```

time: 280 us -> 96.6 us (0.34)
  Pallas kernels: 0 us -> 94.2 us
  waiting for transfers between devices: 68.9 us -> 0 us
  matrix products: 51.9 us -> 0 us
  local copies, waits for them, and re-layouts: 45.6 us -> 2.26 us
  blocking collectives: 35.3 us -> 0 us
  starting transfers between devices: 33.1 us -> 0 us
  other arithmetic: 29.5 us -> 0 us
  between operations: 13.8 us -> 0.01 us
    pallas_call x0 -> x1, Pallas kernels: none -> 94.2 us  [body(): pl.pallas_call(kernel, out_shape=jax.ShapeDtypeStruct((frames_here, rows_...]
    dot_general x12 -> x0, matrix products: 51.9 us -> none  [the longest x3 19.6 us: attend(): jnp.einsum('kgnm,mkd->nkgd', weights, value_heads, preferred_element_type...]
    all_gather x2 -> x0, waiting for transfers between devices: 40.7 us -> none  [the longest x1 26.5 us: body(): lax.all_gather(values, 'band', axis=1, tiled=True)]
    all_to_all x1 -> x0, blocking collectives: 35.3 us -> none  [body(): lax.all_to_all(time_att, 'frames', split_axis=0, concat_axis=1, tiled=True)]
    all_to_all x3 -> x0, starting transfers between devices: 33.1 us -> none  [the longest x1 13.2 us: body(): lax.all_to_all(time_k.reshape(frames_here, rows_here, -1), 'frames', spli...]
    all_to_all x3 -> x0, waiting for transfers between devices: 28.2 us -> none  [the longest x1 23.5 us: body(): lax.all_to_all(time_q.reshape(frames_here, rows_here, -1), 'frames', spli...]
    reduce_sum x7 -> x0, other arithmetic: 22 us -> none  [the longest x3 18.3 us: attend(): totals = jnp.sum(expos, axis=-1)]
    mul x17 -> x0, local copies, waits for them, and re-layouts: 8.56 us -> none  [the longest x14 5.23 us: rms_rows(): return values * scaled * gain]
  transfers between devices with their start and end apart: 5 -> 0, of which waited for: 5 -> 0; matrix products, arithmetic and copies ran while one was open for 13% -> 0% of each run, Pallas kernels for 0% -> 0%
where the time goes in v1:
time: 96.6 us; the launch traced here: 96.5 us
  Pallas kernels  94.2 us (98%)
  local copies, waits for them, and re-layouts  2.26 us (2%)
    pallas_call x1, Pallas kernels, body(): pl.pallas_call(kernel, out_shape=jax.ShapeDtypeStruct((frames_here, rows_...  94.2 us
    unnamed x1, local copies, waits for them, and re-layouts  2.26 us

profile of v1, /device:TPU:1, one launch (start us, length us, event | category | flops | bytes accessed | tf_op | source)
XLA Modules:
  0.0 96.5 jit_solution(9331436825307323867)
XLA Ops:
  0.0 94.2 %block.1 = bf16[2,256,1024]{2,1,0:T(8,128)(2,1)} custom-call(bf16[512,1024]{1,0:T(8,128)(2,1)} %bitcast.3, f32[8,128]{1,0:T(8,128)} %bitcast.4, bf16[1024,1024]{1,0:T(8,128)(2,1)} %wqs_hbm.1, bf16[1024,512]{1,0:T(8,128)(2,1)} %wkvs_hbm.1, bf16[1024,1024]{1,0:T(8,128)(2,1)} %wos_hbm.1, f32[2,64]{1,0:T(2,128)} %qks_ref.1, f32[8,128]{1,0:T(8,128)} %bitcast.5, ...), custom_call_target="tpu_custom_call" | custom-call | tf_op jit(solution)/shard_map/block/pallas_call | solution.py:346
  94.2 2.3 %copy.13 = bf16[2,256,1024]{2,1,0:T(8,128)(2,1)} copy(bf16[2,256,1024]{2,1,0:T(8,128)(2,1)} %block.1) | data formatting | bytes 2097152

commit v2 on v1

v2 whole, which is shorter than its diff:
```python
import functools

import jax
import jax.numpy as jnp
from jax import lax
from jax.experimental import pallas as pl
from jax.experimental.pallas import tpu as pltpu
from jax.sharding import PartitionSpec as P

HEADS = 16
KV_HEADS = 4
HEAD_DIM = 64
D = 1024
ROWS = 256
HALF = 128
PEERS = 64
POS = 4
MESH = pl.DeviceIdType.MESH
F32 = jnp.float32
BF16 = jnp.bfloat16
EXP_SCALE = 0.125 * 1.4426950408889634


def lane_half(shape):
    return lax.broadcasted_iota(jnp.int32, shape, len(shape) - 1) // HEAD_DIM


def rms_pair(tile, gain, ones_block):
    squares = tile * tile
    high = squares.astype(BF16)
    low = (squares - high.astype(F32)).astype(BF16)
    mean = jnp.dot(jnp.concatenate([high, low], axis=1), ones_block, preferred_element_type=F32)
    return tile * lax.rsqrt(mean + 1e-06) * gain


def head_queries(tile, pair):
    parity = (pair // 2) % 2
    here = lane_half(tile.shape) == parity
    turned = pltpu.roll(tile, HEAD_DIM, 1)
    first, second = (tile, turned) if parity == 0 else (turned, tile)
    zero = jnp.zeros_like(tile)
    return jnp.where(here, first, zero).astype(BF16), jnp.where(here, second, zero).astype(BF16)


def join_heads(first, second, parity):
    low = lane_half(first.shape) == 0
    if parity == 0:
        turned = pltpu.roll(second, HEAD_DIM, 1)
        over, under = jnp.where(low, first, turned), jnp.where(low, pltpu.roll(first, HEAD_DIM, 1), second)
    else:
        turned = pltpu.roll(first, HEAD_DIM, 1)
        over, under = jnp.where(low, turned, second), jnp.where(low, first, pltpu.roll(second, HEAD_DIM, 1))
    return over / under


def with_ones(tile, parity):
    return jnp.where(lane_half(tile.shape) == parity, tile, jnp.ones_like(tile))


def both_sides(tile):
    low = lane_half(tile.shape) == 0
    turned = pltpu.roll(tile, HEAD_DIM, 1)
    zero = jnp.zeros_like(tile)
    return (
        (jnp.where(low, tile, zero).astype(BF16), jnp.where(low, zero, turned).astype(BF16)),
        (jnp.where(low, turned, zero).astype(BF16), jnp.where(low, zero, tile).astype(BF16)),
    )


def pack_rows(left, right):
    peers = left.shape[0] // POS
    left = left.reshape(peers // 2, 8, 128)
    right = right.reshape(peers // 2, 8, 128)
    low = lax.broadcasted_iota(jnp.int32, left.shape, 1) < 4
    even = jnp.where(low, left, pltpu.roll(right, 4, 1))
    odd = jnp.where(low, pltpu.roll(left, 4, 1), right)
    return jnp.stack([even, odd], axis=1).reshape(peers, 8, 128)


def unpack_rows(packed):
    peers = packed.shape[0]
    packed = packed.reshape(peers // 2, 2, 8, 128)
    even, odd = packed[:, 0], packed[:, 1]
    low = lax.broadcasted_iota(jnp.int32, even.shape, 1) < 4
    left = jnp.where(low, even, pltpu.roll(odd, 4, 1))
    right = jnp.where(low, pltpu.roll(even, 4, 1), odd)
    return left.reshape(peers * POS, 128), right.reshape(peers * POS, 128)


def gain_row(ref):
    return jnp.concatenate([ref[k : k + 1, :] for k in range(8)], axis=1)


def normalise(values, gain):
    return (values * lax.rsqrt(jnp.mean(values * values, axis=-1, keepdims=True) + 1e-06) * gain).astype(BF16)


def kernel(
    tok_hbm, ns_ref, wqs_hbm, wkvs_hbm, wos_hbm, qks_ref, nt_ref, wqt_hbm, wkvt_hbm, wot_hbm, qkt_ref,
    out_hbm,
    tok, wqs, wkvs, wos, wqt, wkvt, wot,
    normed, queries, kv_all, keys_t, vals, att, send_buf, recv_buf,
    shuffle, stream_t, normed_t, queries_t, keys_time, vals_time, att_t, back_buf, home_buf, out_buf,
    load_sem, kv_send, kv_recv, a2a_send, a2a_recv, back_send, back_recv, out_sem,
):
    me = lax.axis_index("frames")
    band = lax.axis_index("band")
    my_pair = lax.div(me, 2)
    my_half = lax.rem(lax.rem(me, 2) + lax.div(my_pair, 8) + lax.rem(my_pair, 8), 2)

    def peer_of(pair, half):
        return 2 * pair + lax.rem(half + lax.div(pair, 8) + lax.rem(pair, 8), 2)

    core_peer = lax.bitwise_xor(band, 1)
    chip_peer = lax.bitwise_xor(band, 2)

    loads = {}
    for k, (name, src, dst) in enumerate(
        [("tok", tok_hbm, tok), ("wkvs", wkvs_hbm, wkvs), ("wqs", wqs_hbm, wqs), ("wos", wos_hbm, wos),
         ("wqt", wqt_hbm, wqt), ("wkvt", wkvt_hbm, wkvt), ("wot", wot_hbm, wot)]
    ):
        loads[name] = pltpu.make_async_copy(src, dst, load_sem.at[k])
        loads[name].start()

    barrier = pltpu.get_barrier_semaphore()

    def greet(k, carry):
        pl.semaphore_signal(barrier, inc=1, device_id={"frames": lax.rem(me + k, PEERS)}, device_id_type=MESH)
        return carry

    lax.fori_loop(1, PEERS, greet, 0)
    for peer in (core_peer, chip_peer):
        pl.semaphore_signal(barrier, inc=1, device_id={"band": peer}, device_id_type=MESH)

    row = lax.broadcasted_iota(jnp.int32, (256, 128), 0)
    col = lax.broadcasted_iota(jnp.int32, (256, 128), 1)
    ones_block = jnp.where((row // HEAD_DIM) % 2 == col // HEAD_DIM, 1.0 / HEAD_DIM, 0.0).astype(BF16)

    sides = jnp.where(row // 128 == col // HEAD_DIM, 1.0, 0.0).astype(BF16)
    for j in range(POS):
        for kv in range(KV_HEADS):
            vals_time[j, kv, :, 128:256] = sides

    def pair_gain(ref, k):
        return jnp.concatenate([ref[k : k + 1, :], ref[k : k + 1, :]], axis=1)

    loads["tok"].wait()
    gain_space = gain_row(ns_ref)

    def norm_rows(k, carry):
        rows = pl.ds(pl.multiple_of(k * 64, 64), 64)
        normed[rows, :] = normalise(tok[rows, :].astype(F32), gain_space)
        return carry

    lax.fori_loop(0, 2 * ROWS // 64, norm_rows, 0)

    def kv_copy(frame, slot, kind, peer):
        return pltpu.make_async_remote_copy(
            src_ref=kv_all.at[frame, slot], dst_ref=kv_all.at[frame, slot],
            send_sem=kv_send.at[frame, kind], recv_sem=kv_recv.at[frame, kind],
            device_id={"band": peer}, device_id_type=MESH)

    loads["wkvs"].wait()
    key_gain = pair_gain(qks_ref, 1)
    for frame in range(2):
        rows = slice(frame * ROWS, (frame + 1) * ROWS)
        part = jnp.dot(normed[rows, :], wkvs[...], preferred_element_type=F32)
        for t in range(2):
            tile = part[:, t * 128 : (t + 1) * 128]
            kv_all[frame, band, :, t * 128 : (t + 1) * 128] = rms_pair(tile, key_gain, ones_block).astype(BF16)
        kv_all[frame, band, :, 256:512] = part[:, 256:].astype(BF16)
        if frame == 0:
            pl.semaphore_wait(barrier, PEERS - 1 + 2)
        kv_copy(frame, band, 1, chip_peer).start()
        kv_copy(frame, band, 0, core_peer).start()

    loads["wqs"].wait()
    query_gain = pair_gain(qks_ref, 0)
    for n in range(4):
        part = jnp.dot(normed[...], wqs[:, n * 256 : (n + 1) * 256], preferred_element_type=F32)
        for k in range(2):
            pair = 2 * n + k
            tile = rms_pair(part[:, k * 128 : (k + 1) * 128], query_gain, ones_block)
            first, second = head_queries(tile, pair)
            queries[2 * pair] = first
            queries[2 * pair + 1] = second

    def forward(frame):
        kv_copy(frame, chip_peer, 1, chip_peer).wait_recv()
        kv_copy(frame, chip_peer, 2, core_peer).start()

    def space_keys(frame):
        kv_copy(frame, core_peer, 0, core_peer).wait_recv()
        kv_copy(frame, lax.bitwise_xor(band, 3), 2, core_peer).wait_recv()
        for src in range(4):
            at = slice(src * ROWS, (src + 1) * ROWS)
            for t in range(2):
                keys_t[frame, t, :, at] = kv_all[frame, src, :, t * 128 : (t + 1) * 128].T
                value_tile = kv_all[frame, src, :, 256 + t * 128 : 256 + (t + 1) * 128]
                for parity in range(2):
                    vals[frame, 2 * t + parity, at, :] = with_ones(value_tile, parity)

    def space_half(frame, half):
        start = frame * ROWS + half * HALF

        def scores_of(block):
            t, parity = block // 2, block % 2
            first = 8 * t + 4 * parity
            q = queries[first : first + 4, start : start + HALF, :].reshape(4 * HALF, 128)
            return jnp.dot(q, keys_t[frame, t], preferred_element_type=F32)

        ahead = scores_of(0)
        for block in range(4):
            t, parity = block // 2, block % 2
            scores, ahead = ahead, (scores_of(block + 1) if block < 3 else None)
            largest = jnp.max(scores, axis=-1, keepdims=True)
            weights = jnp.exp2((scores - largest) * EXP_SCALE).astype(BF16)
            done = jnp.dot(weights, vals[frame, block], preferred_element_type=F32)
            for k in range(2):
                att[2 * block + k] = join_heads(
                    done[2 * k * HALF : (2 * k + 1) * HALF], done[(2 * k + 1) * HALF : (2 * k + 2) * HALF], parity
                ).astype(BF16)

    def block_columns(left_ref, w_ref, n):
        left = jnp.concatenate([left_ref[k] for k in range(8)], axis=1)
        return jnp.dot(left, w_ref[:, n * 256 : (n + 1) * 256], preferred_element_type=F32)

    def all_of(buf, dst, frame, send_sem, recv_sem, count=PEERS - 1):
        return pltpu.make_async_remote_copy(
            src_ref=buf.at[frame, pl.ds(0, count)], dst_ref=dst.at[frame, pl.ds(0, count)],
            send_sem=send_sem, recv_sem=recv_sem, device_id={"frames": me}, device_id_type=MESH)

    def out_space(frame, half):
        start = frame * ROWS + half * HALF
        for n in range(2):
            packs = []
            for m in (n, n + 2):
                at = slice(m * 256, (m + 1) * 256)
                stream = tok[start : start + HALF, at].astype(F32) + block_columns(att, wos, m)
                stream = stream.astype(BF16).astype(F32)
                packs.append(pack_rows(stream[:, :128], stream[:, 128:]))
            send_buf[frame, half * 32 : half * 32 + 32, :, n * 128 : (n + 1) * 128] = jnp.concatenate(
                packs, axis=1).astype(BF16)

        def send(k, carry):
            pair = lax.rem(my_pair + k, 32)
            peer = peer_of(pair, half)

            @pl.when(peer != me)
            def _():
                pltpu.make_async_remote_copy(
                    src_ref=send_buf.at[frame, half * 32 + pair], dst_ref=recv_buf.at[frame, me],
                    send_sem=a2a_send.at[frame], recv_sem=a2a_recv.at[frame],
                    device_id={"frames": peer}, device_id_type=MESH).start()

            return carry

        lax.fori_loop(0, 32, send, 0)

        @pl.when(my_half == half)
        def _():
            recv_buf[frame, me] = send_buf[frame, half * 32 + my_pair]

    forward(0)
    space_keys(0)
    space_half(0, 0)
    forward(1)
    loads["wos"].wait()
    out_space(0, 0)
    space_keys(1)
    for frame, half in ((1, 0), (0, 1), (1, 1)):
        space_half(frame, half)
        out_space(frame, half)

    gain_time = gain_row(nt_ref)
    query_gain_t = pair_gain(qkt_ref, 0)
    key_gain_t = pair_gain(qkt_ref, 1)
    for name in ("wqt", "wkvt", "wot"):
        loads[name].wait()

    def arrive(frame):
        all_of(send_buf, recv_buf, frame, a2a_send.at[frame], a2a_recv.at[frame]).wait_recv()
        for n in range(2):
            pack = recv_buf[frame, :, :, n * 128 : (n + 1) * 128].astype(F32)
            for half, m in enumerate((n, n + 2)):
                left, right = unpack_rows(pack[:, half * 8 : (half + 1) * 8, :])
                shuffle[2 * m] = left
                shuffle[2 * m + 1] = right
        for j in range(POS):
            rows = slice(j * 64, (j + 1) * 64)
            values = jnp.concatenate([shuffle[k, pl.ds(j, 64, stride=4), :] for k in range(8)], axis=1)
            stream_t[frame, rows, :] = values.astype(BF16)
            normed_t[rows, :] = normalise(values, gain_time)
        hidden = normed_t[...]
        part = jnp.dot(hidden, wkvt[...], preferred_element_type=F32)
        for t in range(2):
            key_tile = rms_pair(part[:, t * 128 : (t + 1) * 128], key_gain_t, ones_block)
            value_tile = part[:, 256 + t * 128 : 256 + (t + 1) * 128]
            for kv, key_side, value_side in zip((2 * t, 2 * t + 1), both_sides(key_tile), both_sides(value_tile)):
                for side in range(2):
                    for j in range(POS):
                        rows = slice(j * 64, (j + 1) * 64)
                        keep = slice(side * 128 + frame * 64, side * 128 + frame * 64 + 64)
                        keys_time[j, kv, keep, :] = key_side[side][rows]
                        vals_time[j, kv, keep, 0:128] = value_side[side][rows]
        for n in range(4):
            part = jnp.dot(hidden, wqt[:, n * 256 : (n + 1) * 256], preferred_element_type=F32)
            for k in range(2):
                pair = 2 * n + k
                tile = rms_pair(part[:, k * 128 : (k + 1) * 128], query_gain_t, ones_block).astype(BF16)
                for j in range(POS):
                    queries_t[frame, j, pair] = tile[j * 64 : (j + 1) * 64]

    def time_half(frame):
        q_frame = 2 * (lax.broadcasted_iota(jnp.int32, (128, 128), 0) % 64) + frame
        k_row = lax.broadcasted_iota(jnp.int32, (128, 128), 1)
        allowed = q_frame >= 2 * (k_row % 64) + k_row // 64

        for j in range(POS):
            rows = slice(j * 64, (j + 1) * 64)
            for kv in range(KV_HEADS):
                q = queries_t[frame, j, 2 * kv : 2 * kv + 2].reshape(128, 128)
                scores = lax.dot_general(q, keys_time[j, kv], (((1,), (1,)), ((), ())), preferred_element_type=F32)
                weights = []
                for side in range(2):
                    mine = jnp.where(allowed, scores[:, side * 128 : (side + 1) * 128], -1e30)
                    largest = jnp.max(mine, axis=-1, keepdims=True)
                    weights.append(jnp.exp2((mine - largest) * EXP_SCALE).astype(BF16))
                done = jnp.dot(jnp.concatenate(weights, axis=1), vals_time[j, kv], preferred_element_type=F32)
                out = (done[:, :128] / done[:, 128:]).astype(BF16)
                att_t[2 * kv, rows, :] = out[:64]
                att_t[2 * kv + 1, rows, :] = out[64:]
        for n in range(4):
            at = slice(n * 256, (n + 1) * 256)
            mixed = stream_t[frame, :, at].astype(F32) + block_columns(att_t, wot, n)
            mixed = mixed.astype(BF16).astype(F32)
            for j in range(POS):
                for half in range(2):
                    shuffle[2 * n + half, pl.ds(j, 64, stride=4), :] = mixed[
                        j * 64 : (j + 1) * 64, half * 128 : (half + 1) * 128]
        for n in range(2):
            packs = [pack_rows(shuffle[2 * m], shuffle[2 * m + 1]) for m in (n, n + 2)]
            back_buf[frame, :, :, n * 128 : (n + 1) * 128] = jnp.concatenate(packs, axis=1).astype(BF16)

        def send(k, carry):
            peer = lax.rem(me + k, PEERS)
            pltpu.make_async_remote_copy(
                src_ref=back_buf.at[frame, peer], dst_ref=home_buf.at[frame, my_half * 32 + my_pair],
                send_sem=back_send.at[frame], recv_sem=back_recv.at[frame, my_half],
                device_id={"frames": peer}, device_id_type=MESH).start()
            return carry

        lax.fori_loop(1, PEERS, send, 0)
        home_buf[frame, my_half * 32 + my_pair] = back_buf[frame, me]

    arrive(0)
    arrive(1)
    time_half(0)
    time_half(1)

    def finish(frame, half):
        for count in (31, 32):
            @pl.when(my_half == half if count == 31 else my_half != half)
            def _():
                all_of(back_buf, home_buf, frame, back_send.at[frame], back_recv.at[frame, half], count).wait_recv()

        rows = slice(half * HALF, (half + 1) * HALF)
        for n in range(2):
            pack = home_buf[frame, half * 32 : half * 32 + 32, :, n * 128 : (n + 1) * 128].astype(F32)
            for part, m in enumerate((n, n + 2)):
                left, right = unpack_rows(pack[:, part * 8 : (part + 1) * 8, :])
                out_buf[frame, rows, m * 256 : m * 256 + 128] = left.astype(BF16)
                out_buf[frame, rows, m * 256 + 128 : (m + 1) * 256] = right.astype(BF16)
        copy = pltpu.make_async_copy(out_buf.at[frame, rows], out_hbm.at[frame, rows], out_sem.at[frame, half])
        copy.start()
        return copy

    copies = [finish(0, 0), finish(1, 0), finish(0, 1), finish(1, 1)]
    for frame in range(2):
        kv_copy(frame, band, 0, core_peer).wait_send()
        kv_copy(frame, band, 1, chip_peer).wait_send()
        kv_copy(frame, chip_peer, 2, core_peer).wait_send()
        all_of(send_buf, recv_buf, frame, a2a_send.at[frame], a2a_recv.at[frame]).wait_send()
        all_of(back_buf, home_buf, frame, back_send.at[frame], back_recv.at[frame, 0]).wait_send()
    for copy in copies:
        copy.wait()


def body(tokens, norm_space, query_space, keyval_space, out_space, qk_space,
         norm_time, query_time, keyval_time, out_time, qk_time):
    frames_here, rows_here, width = tokens.shape
    any_spec = pl.BlockSpec(memory_space=pl.ANY)
    vmem = pl.BlockSpec(memory_space=pltpu.VMEM)
    dma = pltpu.SemaphoreType.DMA
    return pl.pallas_call(
        kernel,
        out_shape=jax.ShapeDtypeStruct((frames_here, rows_here, width), BF16),
        in_specs=[any_spec, vmem, any_spec, any_spec, any_spec, vmem, vmem, any_spec, any_spec, any_spec, vmem],
        out_specs=any_spec,
        scratch_shapes=[
            pltpu.VMEM((2 * ROWS, D), BF16),
            pltpu.VMEM((D, D), BF16), pltpu.VMEM((D, 512), BF16), pltpu.VMEM((D, D), BF16),
            pltpu.VMEM((D, D), BF16), pltpu.VMEM((D, 512), BF16), pltpu.VMEM((D, D), BF16),
            pltpu.VMEM((2 * ROWS, D), BF16),
            pltpu.VMEM((HEADS, 2 * ROWS, 128), BF16),
            pltpu.VMEM((2, 4, ROWS, 512), BF16),
            pltpu.VMEM((2, 2, 128, 4 * ROWS), BF16),
            pltpu.VMEM((2, KV_HEADS, 4 * ROWS, 128), BF16),
            pltpu.VMEM((8, HALF, 128), BF16),
            pltpu.VMEM((2, PEERS, 16, 256), BF16),
            pltpu.VMEM((2, PEERS, 16, 256), BF16),
            pltpu.VMEM((8, ROWS, 128), F32),
            pltpu.VMEM((2, ROWS, D), BF16),
            pltpu.VMEM((ROWS, D), BF16),
            pltpu.VMEM((2, POS, HEADS // 2, 64, 128), BF16),
            pltpu.VMEM((POS, KV_HEADS, 256, 128), BF16),
            pltpu.VMEM((POS, KV_HEADS, 256, 256), BF16),
            pltpu.VMEM((8, ROWS, 128), BF16),
            pltpu.VMEM((2, PEERS, 16, 256), BF16),
            pltpu.VMEM((2, PEERS, 16, 256), BF16),
            pltpu.VMEM((2, ROWS, D), BF16),
            dma((7,)), dma((2, 3)), dma((2, 3)), dma((2,)), dma((2,)), dma((2,)), dma((2, 2)), dma((2, 2)),
        ],
        compiler_params=pltpu.CompilerParams(
            collective_id=0, has_side_effects=True, vmem_limit_bytes=58 * 2**20
        ),
        name="block",
    )(
        tokens.reshape(frames_here * rows_here, width), norm_space.reshape(8, 128), query_space, keyval_space,
        out_space, qk_space, norm_time.reshape(8, 128), query_time, keyval_time, out_time, qk_time,
    )


def solution(mesh):
    placed = (P("frames", "band", None), P(), P(), P(), P(), P(), P(), P(), P(), P(), P())
    return jax.shard_map(
        body, mesh=mesh, in_specs=placed, out_specs=P("frames", "band", None), check_vma=False
    )
```

time: 96.6 us -> 83.9 us (0.87)
  Pallas kernels: 94.2 us -> 81.5 us
    pallas_call x1, Pallas kernels: 94.2 us -> 81.5 us  [body(): pl.pallas_call(kernel, out_shape=jax.ShapeDtypeStruct((frames_here, rows_...]
where the time goes in v2:
time: 83.9 us; the launch traced here: 83.8 us
  Pallas kernels  81.5 us (97%)
  local copies, waits for them, and re-layouts  2.26 us (3%)
    pallas_call x1, Pallas kernels, body(): pl.pallas_call(kernel, out_shape=jax.ShapeDtypeStruct((frames_here, rows_...  81.5 us
    unnamed x1, local copies, waits for them, and re-layouts  2.26 us

profile of v2, /device:TPU:1, one launch (start us, length us, event | category | flops | bytes accessed | tf_op | source)
XLA Modules:
  0.0 83.8 jit_solution(4140856030871744815)
XLA Ops:
  0.0 81.5 %block.1 = bf16[2,256,1024]{2,1,0:T(8,128)(2,1)} custom-call(bf16[512,1024]{1,0:T(8,128)(2,1)} %bitcast.3, f32[8,128]{1,0:T(8,128)} %bitcast.4, bf16[1024,1024]{1,0:T(8,128)(2,1)} %wqs_hbm.1, bf16[1024,512]{1,0:T(8,128)(2,1)} %wkvs_hbm.1, bf16[1024,1024]{1,0:T(8,128)(2,1)} %wos_hbm.1, f32[2,64]{1,0:T(2,128)} %qks_ref.1, f32[8,128]{1,0:T(8,128)} %bitcast.5, ...), custom_call_target="tpu_custom_call" | custom-call | tf_op jit(solution)/shard_map/block/pallas_call | solution.py:395
  81.5 2.3 %copy.13 = bf16[2,256,1024]{2,1,0:T(8,128)(2,1)} copy(bf16[2,256,1024]{2,1,0:T(8,128)(2,1)} %block.1) | data formatting | bytes 2097152

commit v3 on v2

--- a/solution.py
+++ b/solution.py
@@ -120,7 +120,8 @@
          ("wqt", wqt_hbm, wqt), ("wkvt", wkvt_hbm, wkvt), ("wot", wot_hbm, wot)]
     ):
         loads[name] = pltpu.make_async_copy(src, dst, load_sem.at[k])
-        loads[name].start()
+    loads["tok"].start()
+    loads["wkvs"].start()
 
     barrier = pltpu.get_barrier_semaphore()
 
@@ -147,32 +148,36 @@
     loads["tok"].wait()
     gain_space = gain_row(ns_ref)
 
-    def norm_rows(k, carry):
-        rows = pl.ds(pl.multiple_of(k * 64, 64), 64)
-        normed[rows, :] = normalise(tok[rows, :].astype(F32), gain_space)
-        return carry
-
-    lax.fori_loop(0, 2 * ROWS // 64, norm_rows, 0)
-
-    def kv_copy(frame, slot, kind, peer):
+    for name in ("wqs", "wos", "wqt", "wkvt", "wot"):
+        loads[name].start()
+
+    def kv_copy(frame, t, slot, kind, peer):
         return pltpu.make_async_remote_copy(
-            src_ref=kv_all.at[frame, slot], dst_ref=kv_all.at[frame, slot],
-            send_sem=kv_send.at[frame, kind], recv_sem=kv_recv.at[frame, kind],
+            src_ref=kv_all.at[frame, t, slot], dst_ref=kv_all.at[frame, t, slot],
+            send_sem=kv_send.at[frame, t, kind], recv_sem=kv_recv.at[frame, t, kind],
             device_id={"band": peer}, device_id_type=MESH)
 
-    loads["wkvs"].wait()
     key_gain = pair_gain(qks_ref, 1)
     for frame in range(2):
+        def norm_rows(k, carry):
+            rows = pl.ds(pl.multiple_of(frame * ROWS + k * 64, 64), 64)
+            normed[rows, :] = normalise(tok[rows, :].astype(F32), gain_space)
+            return carry
+
+        lax.fori_loop(0, ROWS // 64, norm_rows, 0)
+        if frame == 0:
+            loads["wkvs"].wait()
         rows = slice(frame * ROWS, (frame + 1) * ROWS)
         part = jnp.dot(normed[rows, :], wkvs[...], preferred_element_type=F32)
         for t in range(2):
             tile = part[:, t * 128 : (t + 1) * 128]
-            kv_all[frame, band, :, t * 128 : (t + 1) * 128] = rms_pair(tile, key_gain, ones_block).astype(BF16)
-        kv_all[frame, band, :, 256:512] = part[:, 256:].astype(BF16)
+            kv_all[frame, t, band, :, 0:128] = rms_pair(tile, key_gain, ones_block).astype(BF16)
+            kv_all[frame, t, band, :, 128:256] = part[:, 256 + t * 128 : 256 + (t + 1) * 128].astype(BF16)
         if frame == 0:
             pl.semaphore_wait(barrier, PEERS - 1 + 2)
-        kv_copy(frame, band, 1, chip_peer).start()
-        kv_copy(frame, band, 0, core_peer).start()
+        for t in range(2):
+            kv_copy(frame, t, band, 1, chip_peer).start()
+            kv_copy(frame, t, band, 0, core_peer).start()
 
     loads["wqs"].wait()
     query_gain = pair_gain(qks_ref, 0)
@@ -185,39 +190,38 @@
             queries[2 * pair] = first
             queries[2 * pair + 1] = second
 
-    def forward(frame):
-        kv_copy(frame, chip_peer, 1, chip_peer).wait_recv()
-        kv_copy(frame, chip_peer, 2, core_peer).start()
-
-    def space_keys(frame):
-        kv_copy(frame, core_peer, 0, core_peer).wait_recv()
-        kv_copy(frame, lax.bitwise_xor(band, 3), 2, core_peer).wait_recv()
-        for src in range(4):
-            at = slice(src * ROWS, (src + 1) * ROWS)
-            for t in range(2):
-                keys_t[frame, t, :, at] = kv_all[frame, src, :, t * 128 : (t + 1) * 128].T
-                value_tile = kv_all[frame, src, :, 256 + t * 128 : 256 + (t + 1) * 128]
-                for parity in range(2):
-                    vals[frame, 2 * t + parity, at, :] = with_ones(value_tile, parity)
-
-    def space_half(frame, half):
+    def forward(frame, t):
+        kv_copy(frame, t, chip_peer, 1, chip_peer).wait_recv()
+        kv_copy(frame, t, chip_peer, 2, core_peer).start()
+
+    def space_keys(frame, t):
+        kv_copy(frame, t, core_peer, 0, core_peer).wait_recv()
+        for k in range(4):
+            src = lax.bitwise_xor(band, k)
+            if k == 3:
+                kv_copy(frame, t, src, 2, core_peer).wait_recv()
+            at = slice(k * ROWS, (k + 1) * ROWS)
+            keys_t[frame, t, :, at] = kv_all[frame, t, src, :, 0:128].T
+            value_tile = kv_all[frame, t, src, :, 128:256]
+            for parity in range(2):
+                vals[frame, 2 * t + parity, at, :] = with_ones(value_tile, parity)
+
+    def space_half(frame, half, blocks):
         start = frame * ROWS + half * HALF
 
         def scores_of(block):
-            t, parity = block // 2, block % 2
-            first = 8 * t + 4 * parity
-            q = queries[first : first + 4, start : start + HALF, :].reshape(4 * HALF, 128)
-            return jnp.dot(q, keys_t[frame, t], preferred_element_type=F32)
-
-        ahead = scores_of(0)
-        for block in range(4):
-            t, parity = block // 2, block % 2
-            scores, ahead = ahead, (scores_of(block + 1) if block < 3 else None)
+            q = queries[4 * block : 4 * block + 4, start : start + HALF, :].reshape(4 * HALF, 128)
+            return jnp.dot(q, keys_t[frame, block // 2], preferred_element_type=F32)
+
+        ahead = scores_of(blocks[0])
+        for block in blocks:
+            parity = block % 2
+            scores, ahead = ahead, (scores_of(block + 1) if block != blocks[-1] else None)
             largest = jnp.max(scores, axis=-1, keepdims=True)
             weights = jnp.exp2((scores - largest) * EXP_SCALE).astype(BF16)
             done = jnp.dot(weights, vals[frame, block], preferred_element_type=F32)
             for k in range(2):
-                att[2 * block + k] = join_heads(
+                att[half, 2 * block + k] = join_heads(
                     done[2 * k * HALF : (2 * k + 1) * HALF], done[(2 * k + 1) * HALF : (2 * k + 2) * HALF], parity
                 ).astype(BF16)
 
@@ -236,7 +240,7 @@
             packs = []
             for m in (n, n + 2):
                 at = slice(m * 256, (m + 1) * 256)
-                stream = tok[start : start + HALF, at].astype(F32) + block_columns(att, wos, m)
+                stream = tok[start : start + HALF, at].astype(F32) + block_columns(att.at[half], wos, m)
                 stream = stream.astype(BF16).astype(F32)
                 packs.append(pack_rows(stream[:, :128], stream[:, 128:]))
             send_buf[frame, half * 32 : half * 32 + 32, :, n * 128 : (n + 1) * 128] = jnp.concatenate(
@@ -261,16 +265,24 @@
         def _():
             recv_buf[frame, me] = send_buf[frame, half * 32 + my_pair]
 
-    forward(0)
-    space_keys(0)
-    space_half(0, 0)
-    forward(1)
+    forward(0, 0)
+    space_keys(0, 0)
+    space_half(0, 0, (0, 1))
+    forward(0, 1)
+    space_half(0, 1, (0, 1))
+    space_keys(0, 1)
+    space_half(0, 0, (2, 3))
     loads["wos"].wait()
     out_space(0, 0)
-    space_keys(1)
-    for frame, half in ((1, 0), (0, 1), (1, 1)):
-        space_half(frame, half)
-        out_space(frame, half)
+    forward(1, 0)
+    space_half(0, 1, (2, 3))
+    out_space(0, 1)
+    forward(1, 1)
+    space_keys(1, 0)
+    space_keys(1, 1)
+    for half in range(2):
+        space_half(1, half, (0, 1, 2, 3))
+        out_space(1, half)
 
     gain_time = gain_row(nt_ref)
     query_gain_t = pair_gain(qkt_ref, 0)
@@ -377,9 +389,10 @@
 
     copies = [finish(0, 0), finish(1, 0), finish(0, 1), finish(1, 1)]
     for frame in range(2):
-        kv_copy(frame, band, 0, core_peer).wait_send()
-        kv_copy(frame, band, 1, chip_peer).wait_send()
-        kv_copy(frame, chip_peer, 2, core_peer).wait_send()
+        for t in range(2):
+            kv_copy(frame, t, band, 0, core_peer).wait_send()
+            kv_copy(frame, t, band, 1, chip_peer).wait_send()
+            kv_copy(frame, t, chip_peer, 2, core_peer).wait_send()
         all_of(send_buf, recv_buf, frame, a2a_send.at[frame], a2a_recv.at[frame]).wait_send()
         all_of(back_buf, home_buf, frame, back_send.at[frame], back_recv.at[frame, 0]).wait_send()
     for copy in copies:
@@ -403,10 +416,10 @@
             pltpu.VMEM((D, D), BF16), pltpu.VMEM((D, 512), BF16), pltpu.VMEM((D, D), BF16),
             pltpu.VMEM((2 * ROWS, D), BF16),
             pltpu.VMEM((HEADS, 2 * ROWS, 128), BF16),
-            pltpu.VMEM((2, 4, ROWS, 512), BF16),
+            pltpu.VMEM((2, 2, 4, ROWS, 256), BF16),
             pltpu.VMEM((2, 2, 128, 4 * ROWS), BF16),
             pltpu.VMEM((2, KV_HEADS, 4 * ROWS, 128), BF16),
-            pltpu.VMEM((8, HALF, 128), BF16),
+            pltpu.VMEM((2, 8, HALF, 128), BF16),
             pltpu.VMEM((2, PEERS, 16, 256), BF16),
             pltpu.VMEM((2, PEERS, 16, 256), BF16),
             pltpu.VMEM((8, ROWS, 128), F32),
@@ -419,7 +432,7 @@
             pltpu.VMEM((2, PEERS, 16, 256), BF16),
             pltpu.VMEM((2, PEERS, 16, 256), BF16),
             pltpu.VMEM((2, ROWS, D), BF16),
-            dma((7,)), dma((2, 3)), dma((2, 3)), dma((2,)), dma((2,)), dma((2,)), dma((2, 2)), dma((2, 2)),
+            dma((7,)), dma((2, 2, 3)), dma((2, 2, 3)), dma((2,)), dma((2,)), dma((2,)), dma((2, 2)), dma((2, 2)),
         ],
         compiler_params=pltpu.CompilerParams(
             collective_id=0, has_side_effects=True, vmem_limit_bytes=58 * 2**20

time: 83.9 us -> 83.6 us (level)
  no operation moved by 1% of the time
where the time goes in v3:
time: 83.6 us; the launch traced here: 83 us
  Pallas kernels  80.7 us (97%)
  local copies, waits for them, and re-layouts  2.26 us (3%)
    pallas_call x1, Pallas kernels, body(): pl.pallas_call(kernel, out_shape=jax.ShapeDtypeStruct((frames_here, rows_...  80.7 us
    unnamed x1, local copies, waits for them, and re-layouts  2.26 us

profile of v3, /device:TPU:1, one launch (start us, length us, event | category | flops | bytes accessed | tf_op | source)
XLA Modules:
  0.0 83.0 jit_solution(4590799332379140152)
XLA Ops:
  0.0 80.7 %block.1 = bf16[2,256,1024]{2,1,0:T(8,128)(2,1)} custom-call(bf16[512,1024]{1,0:T(8,128)(2,1)} %bitcast.3, f32[8,128]{1,0:T(8,128)} %bitcast.4, bf16[1024,1024]{1,0:T(8,128)(2,1)} %wqs_hbm.1, bf16[1024,512]{1,0:T(8,128)(2,1)} %wkvs_hbm.1, bf16[1024,1024]{1,0:T(8,128)(2,1)} %wos_hbm.1, f32[2,64]{1,0:T(2,128)} %qks_ref.1, f32[8,128]{1,0:T(8,128)} %bitcast.5, ...), custom_call_target="tpu_custom_call" | custom-call | tf_op jit(solution)/shard_map/block/pallas_call | solution.py:408
  80.7 2.3 %copy.13 = bf16[2,256,1024]{2,1,0:T(8,128)(2,1)} copy(bf16[2,256,1024]{2,1,0:T(8,128)(2,1)} %block.1) | data formatting | bytes 2097152

commit v4 on v3

--- a/solution.py
+++ b/solution.py
@@ -221,7 +221,7 @@
             weights = jnp.exp2((scores - largest) * EXP_SCALE).astype(BF16)
             done = jnp.dot(weights, vals[frame, block], preferred_element_type=F32)
             for k in range(2):
-                att[half, 2 * block + k] = join_heads(
+                att[2 * frame + half, 2 * block + k] = join_heads(
                     done[2 * k * HALF : (2 * k + 1) * HALF], done[(2 * k + 1) * HALF : (2 * k + 2) * HALF], parity
                 ).astype(BF16)
 
@@ -240,7 +240,7 @@
             packs = []
             for m in (n, n + 2):
                 at = slice(m * 256, (m + 1) * 256)
-                stream = tok[start : start + HALF, at].astype(F32) + block_columns(att.at[half], wos, m)
+                stream = tok[start : start + HALF, at].astype(F32) + block_columns(att.at[2 * frame + half], wos, m)
                 stream = stream.astype(BF16).astype(F32)
                 packs.append(pack_rows(stream[:, :128], stream[:, 128:]))
             send_buf[frame, half * 32 : half * 32 + 32, :, n * 128 : (n + 1) * 128] = jnp.concatenate(
@@ -275,14 +275,15 @@
     loads["wos"].wait()
     out_space(0, 0)
     forward(1, 0)
-    space_half(0, 1, (2, 3))
-    out_space(0, 1)
     forward(1, 1)
     space_keys(1, 0)
     space_keys(1, 1)
-    for half in range(2):
-        space_half(1, half, (0, 1, 2, 3))
-        out_space(1, half)
+    space_half(1, 0, (0, 1, 2, 3))
+    out_space(1, 0)
+    space_half(0, 1, (2, 3))
+    out_space(0, 1)
+    space_half(1, 1, (0, 1, 2, 3))
+    out_space(1, 1)
 
     gain_time = gain_row(nt_ref)
     query_gain_t = pair_gain(qkt_ref, 0)
@@ -419,7 +420,7 @@
             pltpu.VMEM((2, 2, 4, ROWS, 256), BF16),
             pltpu.VMEM((2, 2, 128, 4 * ROWS), BF16),
             pltpu.VMEM((2, KV_HEADS, 4 * ROWS, 128), BF16),
-            pltpu.VMEM((2, 8, HALF, 128), BF16),
+            pltpu.VMEM((4, 8, HALF, 128), BF16),
             pltpu.VMEM((2, PEERS, 16, 256), BF16),
             pltpu.VMEM((2, PEERS, 16, 256), BF16),
             pltpu.VMEM((8, ROWS, 128), F32),

time: 83.6 us -> 84 us (level)
  Pallas kernels: 80.7 us -> 81.6 us
    pallas_call x1, Pallas kernels: 80.7 us -> 81.6 us  [body(): pl.pallas_call(kernel, out_shape=jax.ShapeDtypeStruct((frames_here, rows_...]
where the time goes in v4:
time: 84 us; the launch traced here: 83.8 us
  Pallas kernels  81.6 us (97%)
  local copies, waits for them, and re-layouts  2.26 us (3%)
    pallas_call x1, Pallas kernels, body(): pl.pallas_call(kernel, out_shape=jax.ShapeDtypeStruct((frames_here, rows_...  81.6 us
    unnamed x1, local copies, waits for them, and re-layouts  2.26 us

profile of v4, /device:TPU:1, one launch (start us, length us, event | category | flops | bytes accessed | tf_op | source)
XLA Modules:
  0.0 83.8 jit_solution(13913552650456565729)
XLA Ops:
  0.0 81.6 %block.1 = bf16[2,256,1024]{2,1,0:T(8,128)(2,1)} custom-call(bf16[512,1024]{1,0:T(8,128)(2,1)} %bitcast.3, f32[8,128]{1,0:T(8,128)} %bitcast.4, bf16[1024,1024]{1,0:T(8,128)(2,1)} %wqs_hbm.1, bf16[1024,512]{1,0:T(8,128)(2,1)} %wkvs_hbm.1, bf16[1024,1024]{1,0:T(8,128)(2,1)} %wos_hbm.1, f32[2,64]{1,0:T(2,128)} %qks_ref.1, f32[8,128]{1,0:T(8,128)} %bitcast.5, ...), custom_call_target="tpu_custom_call" | custom-call | tf_op jit(solution)/shard_map/block/pallas_call | solution.py:409
  81.6 2.3 %copy.13 = bf16[2,256,1024]{2,1,0:T(8,128)(2,1)} copy(bf16[2,256,1024]{2,1,0:T(8,128)(2,1)} %block.1) | data formatting | bytes 2097152

commit v5 on v3

--- a/solution.py
+++ b/solution.py
@@ -97,11 +97,11 @@
 
 def kernel(
     tok_hbm, ns_ref, wqs_hbm, wkvs_hbm, wos_hbm, qks_ref, nt_ref, wqt_hbm, wkvt_hbm, wot_hbm, qkt_ref,
-    out_hbm,
+    home,
     tok, wqs, wkvs, wos, wqt, wkvt, wot,
     normed, queries, kv_all, keys_t, vals, att, send_buf, recv_buf,
-    shuffle, stream_t, normed_t, queries_t, keys_time, vals_time, att_t, back_buf, home_buf, out_buf,
-    load_sem, kv_send, kv_recv, a2a_send, a2a_recv, back_send, back_recv, out_sem,
+    shuffle, stream_t, normed_t, queries_t, keys_time, vals_time, att_t, back_buf,
+    load_sem, kv_send, kv_recv, a2a_send, a2a_recv, back_send, back_recv, own_sem,
 ):
     me = lax.axis_index("frames")
     band = lax.axis_index("band")
@@ -357,46 +357,38 @@
         def send(k, carry):
             peer = lax.rem(me + k, PEERS)
             pltpu.make_async_remote_copy(
-                src_ref=back_buf.at[frame, peer], dst_ref=home_buf.at[frame, my_half * 32 + my_pair],
-                send_sem=back_send.at[frame], recv_sem=back_recv.at[frame, my_half],
+                src_ref=back_buf.at[frame, peer], dst_ref=home.at[frame, my_half * 32 + my_pair],
+                send_sem=back_send.at[frame], recv_sem=back_recv.at[frame],
                 device_id={"frames": peer}, device_id_type=MESH).start()
             return carry
 
         lax.fori_loop(1, PEERS, send, 0)
-        home_buf[frame, my_half * 32 + my_pair] = back_buf[frame, me]
+        own = pltpu.make_async_copy(
+            back_buf.at[frame, me], home.at[frame, my_half * 32 + my_pair], own_sem.at[frame])
+        own.start()
+        return own
 
     arrive(0)
     arrive(1)
-    time_half(0)
-    time_half(1)
-
-    def finish(frame, half):
-        for count in (31, 32):
-            @pl.when(my_half == half if count == 31 else my_half != half)
-            def _():
-                all_of(back_buf, home_buf, frame, back_send.at[frame], back_recv.at[frame, half], count).wait_recv()
-
-        rows = slice(half * HALF, (half + 1) * HALF)
-        for n in range(2):
-            pack = home_buf[frame, half * 32 : half * 32 + 32, :, n * 128 : (n + 1) * 128].astype(F32)
-            for part, m in enumerate((n, n + 2)):
-                left, right = unpack_rows(pack[:, part * 8 : (part + 1) * 8, :])
-                out_buf[frame, rows, m * 256 : m * 256 + 128] = left.astype(BF16)
-                out_buf[frame, rows, m * 256 + 128 : (m + 1) * 256] = right.astype(BF16)
-        copy = pltpu.make_async_copy(out_buf.at[frame, rows], out_hbm.at[frame, rows], out_sem.at[frame, half])
-        copy.start()
-        return copy
-
-    copies = [finish(0, 0), finish(1, 0), finish(0, 1), finish(1, 1)]
+    own = [time_half(0), time_half(1)]
+
     for frame in range(2):
         for t in range(2):
             kv_copy(frame, t, band, 0, core_peer).wait_send()
             kv_copy(frame, t, band, 1, chip_peer).wait_send()
             kv_copy(frame, t, chip_peer, 2, core_peer).wait_send()
         all_of(send_buf, recv_buf, frame, a2a_send.at[frame], a2a_recv.at[frame]).wait_send()
-        all_of(back_buf, home_buf, frame, back_send.at[frame], back_recv.at[frame, 0]).wait_send()
-    for copy in copies:
-        copy.wait()
+        all_of(back_buf, home, frame, back_send.at[frame], back_recv.at[frame]).wait()
+        own[frame].wait()
+
+
+def place_kernel(home_ref, out_ref):
+    for n in range(2):
+        pack = home_ref[0, :, :, n * 128 : (n + 1) * 128].astype(F32)
+        for part, m in enumerate((n, n + 2)):
+            left, right = unpack_rows(pack[:, part * 8 : (part + 1) * 8, :])
+            out_ref[0, :, m * 256 : m * 256 + 128] = left.astype(BF16)
+            out_ref[0, :, m * 256 + 128 : (m + 1) * 256] = right.astype(BF16)
 
 
 def body(tokens, norm_space, query_space, keyval_space, out_space, qk_space,
@@ -405,9 +397,9 @@
     any_spec = pl.BlockSpec(memory_space=pl.ANY)
     vmem = pl.BlockSpec(memory_space=pltpu.VMEM)
     dma = pltpu.SemaphoreType.DMA
-    return pl.pallas_call(
+    home = pl.pallas_call(
         kernel,
-        out_shape=jax.ShapeDtypeStruct((frames_here, rows_here, width), BF16),
+        out_shape=jax.ShapeDtypeStruct((2, PEERS, 16, 256), BF16),
         in_specs=[any_spec, vmem, any_spec, any_spec, any_spec, vmem, vmem, any_spec, any_spec, any_spec, vmem],
         out_specs=any_spec,
         scratch_shapes=[
@@ -430,9 +422,7 @@
             pltpu.VMEM((POS, KV_HEADS, 256, 256), BF16),
             pltpu.VMEM((8, ROWS, 128), BF16),
             pltpu.VMEM((2, PEERS, 16, 256), BF16),
-            pltpu.VMEM((2, PEERS, 16, 256), BF16),
-            pltpu.VMEM((2, ROWS, D), BF16),
-            dma((7,)), dma((2, 2, 3)), dma((2, 2, 3)), dma((2,)), dma((2,)), dma((2,)), dma((2, 2)), dma((2, 2)),
+            dma((7,)), dma((2, 2, 3)), dma((2, 2, 3)), dma((2,)), dma((2,)), dma((2,)), dma((2,)), dma((2,)),
         ],
         compiler_params=pltpu.CompilerParams(
             collective_id=0, has_side_effects=True, vmem_limit_bytes=58 * 2**20
@@ -442,6 +432,14 @@
         tokens.reshape(frames_here * rows_here, width), norm_space.reshape(8, 128), query_space, keyval_space,
         out_space, qk_space, norm_time.reshape(8, 128), query_time, keyval_time, out_time, qk_time,
     )
+    return pl.pallas_call(
+        place_kernel,
+        out_shape=jax.ShapeDtypeStruct((frames_here, rows_here, width), BF16),
+        grid=(2, 2),
+        in_specs=[pl.BlockSpec((1, 32, 16, 256), lambda f, h: (f, h, 0, 0))],
+        out_specs=pl.BlockSpec((1, HALF, D), lambda f, h: (f, h, 0)),
+        name="place",
+    )(home)
 
 
 def solution(mesh):

time: 83.6 us -> 84.1 us (level)
  Pallas kernels: 80.7 us -> 83.5 us
  local copies, waits for them, and re-layouts: 2.26 us -> 0 us
    pallas_call x1 -> x2, Pallas kernels: 80.7 us -> 83.5 us  [the longest x1 80 us: body(): pl.pallas_call(kernel, out_shape=jax.ShapeDtypeStruct((2, PEERS, 16, 256)...]
    unnamed x1 -> x0, local copies, waits for them, and re-layouts: 2.26 us -> none
where the time goes in v5:
time: 84.1 us; the launch traced here: 83.5 us
  Pallas kernels  83.5 us (99%)
    pallas_call x1, Pallas kernels, body(): pl.pallas_call(kernel, out_shape=jax.ShapeDtypeStruct((2, PEERS, 16, 256)...  80 us
    pallas_call x1, Pallas kernels, body(): pl.pallas_call(place_kernel, out_shape=jax.ShapeDtypeStruct((frames_here,...  3.5 us

profile of v5, /device:TPU:1, one launch (start us, length us, event | category | flops | bytes accessed | tf_op | source)
XLA Modules:
  0.0 83.5 jit_solution(5506218704062963584)
XLA Ops:
  0.0 80.0 %block.1.home_ref = bf16[2,64,16,256]{3,2,1,0:T(8,128)(2,1)} custom-call(bf16[512,1024]{1,0:T(8,128)(2,1)} %bitcast.3, f32[8,128]{1,0:T(8,128)} %bitcast.4, bf16[1024,1024]{1,0:T(8,128)(2,1)} %wqs_hbm.1, bf16[1024,512]{1,0:T(8,128)(2,1)} %wkvs_hbm.1, bf16[1024,1024]{1,0:T(8,128)(2,1)} %wos_hbm.1, f32[2,64]{1,0:T(2,128)} %qks_ref.1, f32[8,128]{1,0:T(8,128)} %bitcast.5, ...), custom_call_target="tpu_custom_call" | custom-call | tf_op jit(solution)/shard_map/block/pallas_call | solution.py:400
  80.0 3.5 %place.1 = bf16[2,256,1024]{2,1,0:T(8,128)(2,1)} custom-call(bf16[2,64,16,256]{3,2,1,0:T(8,128)(2,1)} %block.1.home_ref), custom_call_target="tpu_custom_call" | custom-call | tf_op jit(solution)/shard_map/place/pallas_call | solution.py:435
